TPU v7x, 256 devices: a whole 4x4x8 slice. The times are simulated.
256 devices in a mesh: expert: 64 (over z_lo, y, x, core), helper: 4 (over z_hi).
Axes of the slice: x: 4, y: 4, z: 8 (z_hi: 4, z_lo: 2; z = z_hi * 2 + z_lo), core: 2. Of those that a mesh axis runs over, the one named last changes fastest.
Arguments:
- tokens: bfloat16 [8192, 2048], P(('expert', 'helper')), may hold values from -20 to 20, as said below
- routes: int32 [8192, 8], P(('expert', 'helper')), may hold values from 0 to 127, all different within a row; in each aligned block of 32 rows (0 to 31, 32 to 63, ...) at most 4 rows name the same one
- chosen: int32 [64], replicated, may hold values from 0 to 127, as said below
Outputs:
- hessian: float32 [64, 2048, 2048], P('expert', 'helper')
- inverse: bfloat16 [64, 2048, 2048], P('expert', None, 'helper')
Inputs may be any that keep to these rules, and one draw needn't show every extreme that they name: `routes`: within the 32 rows of one device, no expert is named by more than 4 rows, a bound that some block reaches; every expert is named by some token. `chosen`: the 64 entries are distinct. `tokens`: no row is entirely zero.
All inputs are finite; a program needn't handle non-finite values.
Results may differ from a plain program's by a relative error of at most 0.0025.
Values may be sent and summed in bfloat16 or wider, within the bound.
No kernel may reach another device: no remote copies, remote signals or barrier semaphores. Data moves between devices by JAX's collectives and lax.ppermute only.
A program may use at most 128 MiB of HBM per device.

v0:
```python
import jax
import jax.numpy as jnp
from jax import lax
from jax.sharding import PartitionSpec as P

MOST = 4


highest = lax.Precision.HIGHEST


def matmul(left, right):
    return jnp.dot(left, right, precision=highest, preferred_element_type=jnp.float32)


def local(tokens, routes, chosen):
    slots = chosen.shape[0]
    width = tokens.shape[1]
    flat = routes.reshape(-1)
    hits = (flat[:, None] == chosen[None, :]).astype(jnp.int32)
    before = jnp.cumsum(hits, axis=0) - hits
    slot_base = jnp.arange(slots, dtype=jnp.int32)[None, :] * MOST
    target = jnp.sum(hits * (slot_base + before), axis=1)
    named = jnp.sum(hits, axis=1)
    places = jnp.arange(slots * MOST, dtype=jnp.int32)
    picks = ((places[:, None] == target[None, :]) & (named[None, :] > 0)).astype(jnp.bfloat16)
    picks = jnp.sum(picks.reshape(slots * MOST, routes.shape[0], routes.shape[1]), axis=2)
    outgoing = jnp.dot(picks, tokens, preferred_element_type=jnp.float32).astype(jnp.bfloat16)
    outgoing = outgoing.reshape(slots, MOST, width)
    arrived = lax.all_to_all(outgoing, "expert", split_axis=0, concat_axis=0, tiled=True).reshape(
        -1, width
    )
    live = jnp.sum(jnp.any(arrived != 0, axis=1).astype(jnp.float32))
    helpers = lax.axis_size("helper")
    share = width // helpers
    here = lax.axis_index("helper")
    contract = (((0,), (0,)), ((), ()))
    gram = lax.psum_scatter(
        lax.dot_general(arrived, arrived, contract, preferred_element_type=jnp.float32),
        "helper",
        scatter_dimension=0,
        tiled=True,
    )
    own_block = lax.dynamic_slice_in_dim(gram, here * share, share, 1)
    trace_part = jnp.trace(own_block)
    total_rows, total_trace = lax.psum((live, trace_part), "helper")
    scale = 2.0 / total_rows
    damp = 0.01 * scale * total_trace / width
    row_ids = here * share + jnp.arange(share, dtype=jnp.int32)
    col_ids = jnp.arange(width, dtype=jnp.int32)
    diagonal_rows = (row_ids[:, None] == col_ids[None, :]).astype(jnp.float32)
    hessian = gram * scale + damp * diagonal_rows
    whole = lax.all_gather(hessian, "helper", axis=0, tiled=True)
    block_ids = jnp.arange(share, dtype=jnp.int32)
    block_eye = (block_ids[:, None] == block_ids[None, :]).astype(jnp.float32)
    trailing = whole
    diag_inverses = []
    panel_list = []
    for column in range(helpers):
        diag_block = trailing[:share, :share]
        diag_factor = jnp.linalg.cholesky(diag_block)
        diag_inverse = lax.linalg.triangular_solve(
            diag_factor, block_eye, left_side=True, lower=True
        )
        diag_inverses.append(diag_inverse)
        if column + 1 < helpers:
            panel_rows = matmul(trailing[share:, :share], diag_inverse.T)
            panel_list.append(panel_rows)
            trailing = trailing[share:, share:] - matmul(panel_rows, panel_rows.T)
    right = (col_ids[:, None] == row_ids[None, :]).astype(jnp.float32)
    solved_blocks = []
    for row_block in range(helpers):
        accum = right[row_block * share : (row_block + 1) * share]
        for column in range(row_block):
            offset = (row_block - column - 1) * share
            lower_piece = panel_list[column][offset : offset + share]
            accum = accum - matmul(lower_piece, solved_blocks[column])
        solved_blocks.append(matmul(diag_inverses[row_block], accum))
    solved = jnp.concatenate(solved_blocks, axis=0)
    return (hessian[None], solved.astype(jnp.bfloat16)[None])


def solution(mesh):
    placed = (P(("expert", "helper"), None), P(("expert", "helper"), None), P())
    return jax.shard_map(
        local,
        mesh=mesh,
        in_specs=placed,
        out_specs=(P("expert", "helper", None), P("expert", None, "helper")),
        check_vma=False,
    )
```

profile of v0, /device:TPU:39, one launch (start us, length us, event | category | flops | bytes accessed | tf_op | source)
XLA Modules:
  0.0 1367.3 jit_solution(7755819575388206035)
XLA Ops:
  11.8 24.3 %all_to_all.5 = bf16[64,4,2048]{2,1,0:T(4,128)(2,1)S(1)} all-to-all(bf16[64,4,2048]{2,1,0:T(4,128)(2,1)S(1)} %reshape.158), channel_id=1, replica_groups=mesh['expert'=64,'helper'=4] {'expert'}, dimensions={0} | all-to-all | bytes 2097152 | tf_op jit(solution)/shard_map/all_to_all | solution.py:30
  36.2 9.0 convolution_bitcast_fusion
  47.1 253.9 %reduce-scatter.2.cloned.1.call-done = f32[512,2048]{0,1:T(8,128)} async-done(((f32[2048,2048]{0,1:T(8,128)}), f32[512,2048]{0,1:T(8,128)}) %reduce-scatter.2.cloned.1.call-update) | async-done | bytes 4194320 | tf_op jit(solution)/shard_map/reduce_scatter | solution.py:38
  303.0 32.9 %all-reduce.1 = (f32[]{:T(128)}, f32[]{:T(128)}) all-reduce(f32[]{:T(128)} %convert_reduce_fusion.1, f32[]{:T(128)} %select_reduce_fusion), channel_id=1, replica_groups=mesh['expert'=64,'helper'=4] {'helper'}, use_global_device_ids=true, to_apply=%region_8.9 | all-reduce | flops 2 | bytes 16 | tf_op jit(solution)/shard_map/psum | solution.py:46
  337.2 4.9 select_add_fusion
  348.4 5.8 copy.81
  354.2 293.4 %all-gather.2.cloned.1.call-done = f32[2048,2048]{0,1:T(8,128)} async-done(((f32[512,2048]{0,1:T(8,128)}), f32[2048,2048]{0,1:T(8,128)}) %all-gather.2.cloned.1.call-update) | async-done | bytes 16777232 | tf_op jit(solution)/shard_map/all_gather | solution.py:53
  650.7 11.7 cholesky.462
  662.5 9.8 custom-call.35
  673.0 11.7 cholesky.481
  684.8 10.0 custom-call.36
  695.4 11.7 cholesky.502
  707.8 9.8 custom-call.37
  718.2 11.7 cholesky.519
  734.4 7.9 while.8
  742.2 39.3 %custom-call.38 = f32[4,128,128]{1,2,0:T(8,128)S(1)} custom-call(f32[4,128,128]{2,1,0:T(8,128)S(1)} %get-tuple-element.30), custom_call_target="InvertDiagBlocksLowerTriangular" | custom-call | tf_op jit(solution)/shard_map/triangular_solve/custom-call.3 | solution.py:62
  788.6 12.4 fusion
  810.6 17.4 %slice_subtract_fusion = f32[1536,1536]{0,1:T(8,128)S(1)} fusion(f32[2048,2048]{0,1:T(8,128)S(1)} %bitcast.234, f32[1536,512]{1,0:T(8,128)S(1)} %fusion), kind=kOutput, calls=%fused_computation.8 | convolution fusion | flops 14497873920 | bytes 25165824 | tf_op jit(solution)/shard_map/dot_general | solution.py:13
  828.0 3.6 copy-done.2
  833.5 11.7 cholesky.534
  845.4 9.8 custom-call.39
  855.9 11.7 cholesky.553
  869.0 10.0 custom-call.40
  879.7 11.7 cholesky.574
  892.1 9.8 custom-call.41
  902.5 12.1 cholesky.591
  918.2 8.3 while.9
  926.5 39.3 %custom-call.42 = f32[4,128,128]{1,2,0:T(8,128)S(1)} custom-call(f32[4,128,128]{2,1,0:T(8,128)S(1)} %get-tuple-element.31), custom_call_target="InvertDiagBlocksLowerTriangular" | custom-call | tf_op jit(solution)/shard_map/triangular_solve/custom-call.3 | solution.py:62
  971.4 8.3 fusion.2
  979.6 8.9 slice_subtract_fusion.1
  996.9 11.7 cholesky.606
  1009.8 9.8 custom-call.43
  1023.5 11.7 cholesky.625
  1037.2 10.2 custom-call.44
  1051.4 13.2 cholesky.646
  1066.7 11.3 custom-call.45
  1081.0 11.7 cholesky.663
  1099.7 13.9 %while.10 = (s32[]{:T(128)}, f32[512,512]{1,0:T(8,128)}, s32[4,2]{0,1:T(2,128)S(1)}, f32[4,128,128]{2,1,0:T(8,128)}, s32[]{:T(128)}) while((s32[]{:T(128)}, f32[512,512]{1,0:T(8,128)}, s32[4,2]{0,1:T(2,128)S(1)}, f32[4,128,128]{2,1,0:T(8,128)}, s32[]{:T(128)}) %tuple.120), condition=%wide.while_cond.clone.1, body=%wide.while_body.clone.1.sunk | while | flops 2 | bytes 132705 | solution.py:62
  1113.6 40.7 %custom-call.46 = f32[4,128,128]{1,2,0:T(8,128)} custom-call(f32[4,128,128]{2,1,0:T(8,128)} %get-tuple-element.32), custom_call_target="InvertDiagBlocksLowerTriangular" | custom-call | tf_op jit(solution)/shard_map/triangular_solve/custom-call.3 | solution.py:62
  1178.5 12.1 cholesky.678
  1191.8 9.8 custom-call.47
  1205.5 11.7 cholesky.697
  1219.2 9.8 custom-call.48
  1232.9 13.3 cholesky.718
  1248.4 11.3 custom-call.49
  1262.7 11.7 cholesky.735
  1281.2 13.5 while.11
  1294.7 40.9 %custom-call.50 = f32[4,128,128]{1,2,0:T(8,128)} custom-call(f32[4,128,128]{2,1,0:T(8,128)} %get-tuple-element.33), custom_call_target="InvertDiagBlocksLowerTriangular" | custom-call | tf_op jit(solution)/shard_map/triangular_solve/custom-call.3 | solution.py:62
  (282 shorter events, 192.5 us)
Async XLA Ops:
  7.2 3.8 copy-start
  7.2 293.9 %reduce-scatter.2.cloned.1.call-start = ((), (), s32[]{:S(2)}) async-start(), calls=%async_computation.2 | async-start | bytes 20971520 | tf_op jit(solution)/shard_map/reduce_scatter | solution.py:38
  45.2 602.4 %all-gather.2.cloned.1.call-start = ((), (), s32[]{:S(2)}) async-start(), calls=%async_computation.3 | async-start | bytes 20971520 | tf_op jit(solution)/shard_map/all_gather | solution.py:53
  342.1 3.4 copy-start.3
  786.0 24.6 %slice-start = ((s8[16777216]{0:T(1024)(128)(4,1)}), s8[4194304]{0:T(1024)(128)(4,1)S(1)}, s32[]{:S(2)}) async-start(s8[16777216]{0:T(1024)(128)(4,1)} %bitcast.233), calls=%async_computation.4 | async-start | bytes 8388608
  786.4 14.7 %copy-start.8 = (f32[2048,512]{1,0:T(8,128)S(1)}, f32[2048,512]{1,0:T(8,128)}, u32[]{:S(2)}) copy-start(f32[2048,512]{1,0:T(8,128)} %get-tuple-element.126) | copy-start | bytes 12582916
  788.6 22.0 %slice-start.1 = ((s8[16777216]{0:T(1024)(128)(4,1)}), s8[4194304]{0:T(1024)(128)(4,1)S(1)}, s32[]{:S(2)}) async-start(s8[16777216]{0:T(1024)(128)(4,1)} %bitcast.233), calls=%async_computation.5 | async-start | bytes 8388608
  788.6 22.0 %slice-start.2 = ((s8[16777216]{0:T(1024)(128)(4,1)}), s8[4194304]{0:T(1024)(128)(4,1)S(1)}, s32[]{:S(2)}) async-start(s8[16777216]{0:T(1024)(128)(4,1)} %bitcast.233), calls=%async_computation.6 | async-start | bytes 8388608
  803.9 6.6 slice-start.3
  828.0 3.6 copy-start.2
  967.3 3.4 copy-start.11
  968.7 1.9 copy-start.15
  970.7 0.7 copy-start.24
  988.5 1.9 copy-start.4
  995.9 1.0 copy-start.23
  1022.8 0.7 copy-start.29
  1154.3 11.3 copy-start.5
  1155.8 13.5 copy-start.9
  1158.5 7.1 copy-start.13
  1161.8 7.4 copy-start.17
  1165.7 3.6 copy-start.26
  1169.3 1.0 copy-start.6
  1177.5 1.0 copy-start.22
  1204.8 0.7 copy-start.30
  1335.7 11.1 copy-start.12
  1335.7 11.1 copy-start.16
  1335.7 11.1 copy-start.19
  1335.7 11.1 copy-start.25
  1339.8 9.0 copy-start.21
  1346.8 3.9 copy-start.10
  1346.8 3.9 copy-start.14
  1346.9 3.9 copy-start.18
  1346.9 3.9 copy-start.27
  1348.7 3.9 copy-start.20
  1350.7 3.8 copy-start.7
  1354.5 4.1 copy-start.28
  1354.6 5.5 copy-start.1
Sparse Core Ops, SparseCore 0:
  45.3 255.7 reduce-scatter.1
  342.3 305.2 all-gather.1
where the time goes:
time: 1380 us; the launch traced here: 1370 us
  waiting for transfers between devices  547 us (40%)
  other arithmetic  520 us (38%)
  matrix products  140 us (10%)
  local copies, waits for them, and re-layouts  75.3 us (5%)
  blocking collectives  57.2 us (4%)
  between operations  27 us (2%)
    another operation x59, other arithmetic, local(): diag_factor = jnp.linalg.cholesky(diag_block)  329 us
    all_gather x1, waiting for transfers between devices, local(): whole = lax.all_gather(hessian, 'helper', axis=0, tiled=True)  293 us
    reduce_scatter x1, waiting for transfers between devices, local(): lax.psum_scatter(lax.dot_general(arrived, arrived, contract, preferred_el...  254 us
    another operation x9, other arithmetic, local(): lax.linalg.triangular_solve(diag_factor, block_eye, left_side=True, lower...  166 us
    dot_general x16, matrix products, matmul(): jnp.dot(left, right, precision=highest, preferred_element_type=jnp.float32)  75.7 us
    another operation x53, local copies, waits for them, and re-layouts, local(): lax.linalg.triangular_solve(diag_factor, block_eye, left_side=True, lower...  44.9 us
    psum x1, blocking collectives, local(): total_rows, total_trace = lax.psum((live, trace_part), 'helper')  32.9 us
    another operation x28, matrix products, local(): lax.linalg.triangular_solve(diag_factor, block_eye, left_side=True, lower...  31.8 us
  transfers between devices with their start and end apart: 2, of which 2 were waited for; matrix products, arithmetic and copies ran while one was open for 1% of the time, Pallas kernels for 0%

commit v1 on v0

v1 whole, which is shorter than its diff:
```python
import functools

import jax
import jax.numpy as jnp
from jax import lax
from jax.experimental import pallas as pl
from jax.experimental.pallas import tpu as pltpu
from jax.sharding import PartitionSpec as P

MOST = 4
BLOCK = 128
TILE = 256
CHAIN = 8

f32 = jnp.float32
bf16 = jnp.bfloat16


def at(index, size):
    return pl.ds(pl.multiple_of(index * size, size), size)


def multiply(left, right):
    return jnp.dot(left, right, preferred_element_type=f32)


def pieces(value):
    high = value.astype(bf16)
    rest = value - high.astype(f32)
    middle = rest.astype(bf16)
    return high, middle, (rest - middle.astype(f32)).astype(bf16)


def as_left(value):
    high, middle, low = pieces(value)
    return jnp.concatenate([high, high, middle, middle, high, low], axis=1)


def as_right(value):
    high, middle, low = pieces(value)
    return jnp.concatenate([high, middle, high, middle, low, high], axis=0)


def spread_row(group, row):
    return jnp.broadcast_to(group[row : row + 1, :], group.shape)


def spread_lane(group, lane):
    return jnp.broadcast_to(group[:, lane : lane + 1], group.shape)


def inverse_factor(groups):
    number = len(groups)
    groups = list(groups)
    row = lax.broadcasted_iota(jnp.int32, (8, BLOCK), 0)
    lane = lax.broadcasted_iota(jnp.int32, (8, BLOCK), 1)
    result = []
    for first in range(number):
        columns = [
            [spread_lane(groups[g], CHAIN * first + k) for g in range(first, number)]
            for k in range(CHAIN)
        ]
        norms = []
        for j in range(CHAIN):
            pivot = spread_row(columns[j][0], j)
            scale = 1.0 / pivot
            norms.append(lax.rsqrt(pivot))
            hit = lane == CHAIN * first + j
            pivot_row = jnp.where(hit, 1.0, spread_row(groups[first], j))
            heads = [spread_row(columns[k][0], j) for k in range(j + 1, CHAIN)]
            for g in range(first, number):
                factor = columns[j][g - first] * scale
                below = hit
                if g == first:
                    factor = jnp.where(row > j, factor, 0.0)
                    below = hit & (row > j)
                groups[g] = jnp.where(below, 0.0, groups[g]) - factor * pivot_row
                for k in range(j + 1, CHAIN):
                    columns[k][g - first] -= factor * heads[k - j - 1]
        norm = norms[0]
        for j in range(1, CHAIN):
            norm = jnp.where(row == j, norms[j], norm)
        diagonal = row + CHAIN * first
        unit = jnp.where(lane < diagonal, groups[first], 0.0)
        result.append(jnp.where(lane == diagonal, 1.0, unit) * norm)
    return jnp.concatenate(result, axis=0)


def kernel(here_ref, rows_ref, hessian_ref, inverse_ref, work, upper, lower, turned):
    here = here_ref[0]
    count_rows, width = rows_ref.shape
    share = hessian_ref.shape[0]
    tiles = width // TILE
    share_tiles = share // TILE

    def add_up(i, sums):
        squares, live = sums
        part = rows_ref[at(i, 32), :].astype(f32)
        squares = squares + jnp.sum((part * part).reshape(4, 8, width), axis=0)
        named = jnp.max(jnp.abs(part), axis=1, keepdims=True) > 0.0
        return squares, live + named.astype(f32)

    squares, live = lax.fori_loop(
        0, count_rows // 32, add_up, (jnp.zeros((8, width), f32), jnp.zeros((32, 1), f32))
    )
    scale = 2.0 / jnp.sum(live, axis=0, keepdims=True)
    trace = jnp.sum(jnp.sum(squares, axis=1, keepdims=True), axis=0, keepdims=True)
    damp = 0.01 * scale * trace / width

    def diagonal(first_row, first_column):
        row = lax.broadcasted_iota(jnp.int32, (TILE, TILE), 0) + first_row
        return row == lax.broadcasted_iota(jnp.int32, (TILE, TILE), 1) + first_column

    def hessian_tile(t, first_row):
        gram = multiply(turned[...], rows_ref[:, at(t, TILE)])
        return gram * scale + jnp.where(diagonal(first_row, t * TILE), damp, 0.0)

    def fill(i, carry):
        turned[...] = rows_ref[:, at(i, TILE)].T

        def tile(t, carry):
            work[at(i, TILE), at(t, TILE)] = hessian_tile(t, i * TILE)
            return carry

        lax.fori_loop(i, tiles, tile, 0)
        for t in range(share_tiles):
            unit = diagonal(i * TILE, here * share + t * TILE)
            work[at(i, TILE), pl.ds(width + t * TILE, TILE)] = unit.astype(f32)
        return carry

    lax.fori_loop(0, tiles, fill, 0)

    def own(i, carry):
        block = here * share_tiles + i
        turned[...] = rows_ref[:, at(block, TILE)].T

        def tile(t, carry):
            hessian_ref[at(i, TILE), at(t, TILE)] = hessian_tile(t, block * TILE)
            return carry

        return lax.fori_loop(0, tiles, tile, carry)

    lax.fori_loop(0, share_tiles, own, 0)

    def step(k, carry):
        groups = [
            work[pl.ds(pl.multiple_of(k * BLOCK + 8 * g, 8), 8), at(k, BLOCK)]
            for g in range(BLOCK // 8)
        ]
        solve = as_left(inverse_factor(groups))
        first = (k + 1) // 2

        def panel(t):
            solved = multiply(solve, as_right(work[at(k, BLOCK), at(t, TILE)]))
            upper[:, at(t, TILE)] = as_right(solved)
            return solved

        def factor_tile(t, carry):
            lower[at(t, TILE), :] = as_left(panel(t).T)
            return carry

        def inverse_tile(t, carry):
            inverse_ref[at(k, BLOCK), at(t - tiles, TILE)] = panel(t).astype(bf16)
            return carry

        lax.fori_loop(first, tiles, factor_tile, 0)
        lax.fori_loop(tiles, tiles + share_tiles, inverse_tile, 0)

        def trailing_row(i, carry):
            def tile(t, carry):
                spot = (at(i, TILE), at(t, TILE))
                work[spot] = work[spot] - multiply(lower[at(i, TILE), :], upper[:, at(t, TILE)])
                return carry

            return lax.fori_loop(i, tiles + share_tiles, tile, carry)

        return lax.fori_loop(first, tiles, trailing_row, carry)

    lax.fori_loop(0, width // BLOCK, step, 0)


def factor(here, rows, share):
    count_rows, width = rows.shape
    return pl.pallas_call(
        kernel,
        out_shape=(
            jax.ShapeDtypeStruct((share, width), f32),
            jax.ShapeDtypeStruct((width, share), bf16),
        ),
        in_specs=[
            pl.BlockSpec(memory_space=pltpu.SMEM),
            pl.BlockSpec(memory_space=pltpu.VMEM),
        ],
        out_specs=(pl.BlockSpec(memory_space=pltpu.VMEM),) * 2,
        scratch_shapes=[
            pltpu.VMEM((width, width + share), f32),
            pltpu.VMEM((6 * BLOCK, width + share), bf16),
            pltpu.VMEM((width, 6 * BLOCK), bf16),
            pltpu.VMEM((TILE, count_rows), bf16),
        ],
        compiler_params=pltpu.CompilerParams(vmem_limit_bytes=56 * 2**20),
        name="factor",
    )(here, rows)


def local(tokens, routes, chosen):
    slots = chosen.shape[0]
    width = tokens.shape[1]
    flat = routes.reshape(-1)
    hits = (flat[:, None] == chosen[None, :]).astype(jnp.int32)
    before = jnp.cumsum(hits, axis=0) - hits
    slot_base = jnp.arange(slots, dtype=jnp.int32)[None, :] * MOST
    target = jnp.sum(hits * (slot_base + before), axis=1)
    named = jnp.sum(hits, axis=1)
    places = jnp.arange(slots * MOST, dtype=jnp.int32)
    picks = ((places[:, None] == target[None, :]) & (named[None, :] > 0)).astype(jnp.bfloat16)
    picks = jnp.sum(picks.reshape(slots * MOST, routes.shape[0], routes.shape[1]), axis=2)
    outgoing = jnp.dot(picks, tokens, preferred_element_type=jnp.float32).astype(jnp.bfloat16)
    outgoing = outgoing.reshape(slots, MOST, width)
    arrived = lax.all_to_all(outgoing, "expert", split_axis=0, concat_axis=0, tiled=True).reshape(
        -1, width
    )
    rows = lax.all_gather(arrived, "helper", axis=0, tiled=True)
    here = lax.axis_index("helper").astype(jnp.int32).reshape(1)
    hessian, inverse = factor(here, rows, width // lax.axis_size("helper"))
    return (hessian[None], inverse[None])


def solution(mesh):
    placed = (P(("expert", "helper"), None), P(("expert", "helper"), None), P())
    return jax.shard_map(
        local,
        mesh=mesh,
        in_specs=placed,
        out_specs=(P("expert", "helper", None), P("expert", None, "helper")),
        check_vma=False,
    )
```

time: 1380 us -> 343 us (0.25)
  other arithmetic: 520 us -> 2.37 us
  waiting for transfers between devices: 547 us -> 87.5 us
  Pallas kernels: 0 us -> 211 us
  matrix products: 140 us -> 0.45 us
  local copies, waits for them, and re-layouts: 75.3 us -> 2.82 us
  blocking collectives: 57.2 us -> 24.3 us
    another operation x70 -> x2, other arithmetic: 495 us -> 0.65 us  [the longest x59 329 us: local(): diag_factor = jnp.linalg.cholesky(diag_block)]
    reduce_scatter x1 -> x0, waiting for transfers between devices: 254 us -> none  [local(): lax.psum_scatter(lax.dot_general(arrived, arrived, contract, preferred_el...]
    pallas_call x0 -> x1, Pallas kernels: none -> 211 us  [factor(): pl.pallas_call(kernel, out_shape=(jax.ShapeDtypeStruct((share, width), f3...]
    all_gather x1, waiting for transfers between devices: 293 us -> 87.5 us  [local(): rows = lax.all_gather(arrived, 'helper', axis=0, tiled=True)]
    dot_general x17 -> x0, matrix products: 84.7 us -> none  [the longest x16 75.7 us: matmul(): jnp.dot(left, right, precision=highest, preferred_element_type=jnp.float32)]
    another operation x52 -> x0, matrix products: 54.6 us -> none  [the longest x28 31.8 us: local(): lax.linalg.triangular_solve(diag_factor, block_eye, left_side=True, lower...]
    another operation x71 -> x1, local copies, waits for them, and re-layouts: 48.9 us -> 0.01 us  [the longest x53 44.9 us: local(): lax.linalg.triangular_solve(diag_factor, block_eye, left_side=True, lower...]
    psum x1 -> x0, blocking collectives: 32.9 us -> none  [local(): total_rows, total_trace = lax.psum((live, trace_part), 'helper')]
  transfers between devices with their start and end apart: 2 -> 1, of which waited for: 2 -> 1; matrix products, arithmetic and copies ran while one was open for 1% -> 0% of each run, Pallas kernels for 0% -> 0%
where the time goes in v1:
time: 343 us
  Pallas kernels  211 us (62%)
  waiting for transfers between devices  87.5 us (26%)
  blocking collectives  24.3 us (7%)
  between operations  14.1 us (4%)
    pallas_call x1, Pallas kernels, factor(): pl.pallas_call(kernel, out_shape=(jax.ShapeDtypeStruct((share, width), f3...  211 us
    all_gather x1, waiting for transfers between devices, local(): rows = lax.all_gather(arrived, 'helper', axis=0, tiled=True)  87.5 us
    all_to_all x1, blocking collectives, local(): lax.all_to_all(outgoing, 'expert', split_axis=0, concat_axis=0, tiled=True)  24.3 us
  transfers between devices with their start and end apart: 1, of which 1 were waited for; matrix products, arithmetic and copies ran while one was open for 0% of the time, Pallas kernels for 0%

profile of v1, /device:TPU:39, one launch (start us, length us, event | category | flops | bytes accessed | tf_op | source)
XLA Modules:
  0.0 343.0 jit_solution(14138634575517350884)
XLA Ops:
  7.2 0.0 copy-start
  7.2 0.0 all-gather.2.cloned.1.call-start
  7.2 0.8 copy.8
  8.0 0.1 eq.46
  8.1 0.1 eq.42
  8.2 0.7 compare_convert_fusion
  8.9 0.6 reduce-window.6
  9.5 0.2 slice_reduce_fusion
  9.7 0.8 convert_reduce_fusion
  10.5 0.1 gt.16
  10.6 0.1 eq.50
  10.7 0.2 fusion.2
  10.9 0.0 copy-done
  10.9 0.4 convolution_convert_fusion
  11.4 0.4 reshape.61
  11.8 24.3 %all_to_all.5 = bf16[64,4,2048]{2,1,0:T(4,128)(2,1)S(1)} all-to-all(bf16[64,4,2048]{2,1,0:T(4,128)(2,1)S(1)} %reshape.61), channel_id=1, replica_groups=mesh['expert'=64,'helper'=4] {'expert'}, dimensions={0} | all-to-all | bytes 2097152 | tf_op jit(solution)/shard_map/all_to_all | solution.py:220
  36.1 1.1 reshape.62
  37.2 0.0 all-gather.2.cloned.1.call-update
  37.2 87.5 %all-gather.2.cloned.1.call-done.rows_ref = bf16[1024,2048]{1,0:T(8,128)(2,1)} async-done(((bf16[256,2048]{1,0:T(8,128)(2,1)}), bf16[1024,2048]{1,0:T(8,128)(2,1)}) %all-gather.2.cloned.1.call-update) | async-done | bytes 4194320 | tf_op jit(solution)/shard_map/all_gather | solution.py:223
  124.7 211.5 %factor.1 = (f32[512,2048]{1,0:T(8,128)}, bf16[2048,512]{1,0:T(8,128)(2,1)}) custom-call(s32[1]{0:T(128)} %bitcast.here_ref, bf16[1024,2048]{1,0:T(8,128)(2,1)} %all-gather.2.cloned.1.call-done.rows_ref), custom_call_target="tpu_custom_call" | custom-call | tf_op jit(solution)/shard_map/factor/pallas_call | solution.py:184
  (4 shorter events, 0.1 us)
Async XLA Ops:
  7.2 3.8 %copy-start = (bf16[32,2048]{1,0:T(8,128)(2,1)S(1)}, bf16[32,2048]{1,0:T(8,128)(2,1)}, u32[]{:S(2)}) copy-start(bf16[32,2048]{1,0:T(8,128)(2,1)} %param.3) | copy-start | bytes 393220
  7.2 117.5 %all-gather.2.cloned.1.call-start = ((), (), s32[]{:S(2)}) async-start(), calls=%async_computation.1 | async-start | bytes 5242880 | tf_op jit(solution)/shard_map/all_gather | solution.py:223
Sparse Core Ops, SparseCore 0:
  37.4 87.2 all-gather.1
